TPU v7x, 128 devices: a whole 4x4x4 slice. The times are simulated.
128 devices in a mesh: row: 8 (over x_hi, y), col: 16 (over x_lo, z, core).
Axes of the slice: x: 4 (x_hi: 2, x_lo: 2; x = x_hi * 2 + x_lo), y: 4, z: 4, core: 2. Of those that a mesh axis runs over, the one named last changes fastest.
Arguments:
- counts: int32 [16384, 32768], P('row', 'col'), may hold values from 0 to 64
- row_totals: int32 [16384], P('row'), may hold values from 1000 to 90000
- column_totals: int32 [32768], P('col'), may hold values from 1000 to 60000
- row_vectors: float32 [16384, 256], P(('row', 'col')), may hold values from -0.6 to 0.6
- column_vectors: float32 [32768, 256], P(('col', 'row')), may hold values from -0.6 to 0.6
- row_squares: float32 [16384, 256], P(('row', 'col')), may hold values from 327.68 to 3276.8
- column_squares: float32 [32768, 256], P(('col', 'row')), may hold values from 163.84 to 1638.4
Outputs:
- new_rows: float32 [16384, 256], P(('row', 'col'))
- new_columns: float32 [32768, 256], P(('col', 'row'))
- squares_row: float32 [16384, 256], P(('row', 'col'))
- squares_column: float32 [32768, 256], P(('col', 'row'))
- mean_loss: float32 [], replicated
All inputs are finite; a program needn't handle non-finite values.
Results may differ from a plain program's by a relative error of at most 0.0047.
Values may be sent and summed in bfloat16 or wider, within the bound.
A program may use at most 128 MiB of HBM per device.

v0:
```python
import jax
import jax.numpy as jnp
from jax import lax
from jax.experimental import pallas as pl
from jax.experimental.pallas import tpu as pltpu
from jax.sharding import PartitionSpec as P

F32 = jnp.float32
BF16 = jnp.bfloat16
LOG2E = 1.4426950408889634
LN2 = 0.6931471805599453
SHIFT = 20
K = 256
NR = 2048
NC = 2048
STRIP = 128
SLOTS = 6
TILE = 512
PIECE = 16

R_PARTNER, R_PLUS, R_MINUS, R_FAR, R_PPLUS, R_PMINUS, R_PFAR, R_SPARE, R_SIB, R_PSIB = range(10)
C_PARTNER, C_PLUS, C_MINUS, C_FAR, C_PPLUS, C_PMINUS, C_PFAR = range(10, 17)
G_COLS = 17
G_SIB = 24
G_ROWS = 32
N_SEMS = 40
WIDTH = 768
OWN, NEXT, LAST, CROSS, FAR, CROSS_NEXT, CROSS_LAST, CROSS_FAR = range(8)


def kernel(
    counts, row_totals, column_totals, row_vectors, column_vectors,
    row_grad, column_grad, mean_loss,
    cbuf, lrow, lcol, B, C, rows, rowsT, cols, colsq, rg, cg, cgq, slopes_a, slopes_b, scores_a, scores_b,
    sq_a, sq_b, tq_a, tq_b, lacc,
    csend, cpart, rsend, rsib, rsum, rpart, small, small_in, small_row, small_col,
    csem, ssem, rsem, small_s, small_r,
):
    r = lax.axis_index("row")
    c = lax.axis_index("col")
    hi, y = r // 4, r % 4
    lo, z, core = c // 8, (c // 2) % 4, c % 2

    def row_at(h, yy):
        return h * 4 + (yy + 4) % 4

    def col_at(l, zz, k):
        return l * 8 + ((zz + 4) % 4) * 2 + k

    def remote(src, dst, which, dev):
        return pltpu.make_async_remote_copy(
            src_ref=src, dst_ref=dst, send_sem=ssem.at[which], recv_sem=rsem.at[which],
            device_id=dev, device_id_type=pl.DeviceIdType.MESH)

    def small_copy(src, dst, which, dev):
        return pltpu.make_async_remote_copy(
            src_ref=src, dst_ref=dst, send_sem=small_s.at[which], recv_sem=small_r.at[which],
            device_id=dev, device_id_type=pl.DeviceIdType.MESH)

    def strip(i, slot):
        return pltpu.make_async_copy(
            counts.at[pl.ds(pl.multiple_of(i * STRIP, STRIP), STRIP)], cbuf.at[slot], csem.at[slot])

    for s in range(SLOTS):
        strip(s, s).start()

    barrier = pltpu.get_barrier_semaphore()
    for d in range(1, 8):
        pl.semaphore_signal(barrier, inc=1, device_id=((r + d) % 8, c), device_id_type=pl.DeviceIdType.MESH)
    for d in range(1, 16):
        pl.semaphore_signal(barrier, inc=1, device_id=(r, (c + d) % 16), device_id_type=pl.DeviceIdType.MESH)

    rows[lo, z, core] = row_vectors[...].astype(BF16)
    cols[r] = column_vectors[...].astype(BF16)
    part = jnp.sum(row_totals[...].astype(F32), axis=0, keepdims=True)
    small[0] = jnp.broadcast_to(jnp.sum(part, axis=1, keepdims=True), (8, 128))
    for b in range(16):
        v = jnp.log(row_totals[b:b + 1, :].astype(F32))
        lrow[b * 128:(b + 1) * 128, :] = jnp.transpose(jnp.broadcast_to(v, (128, 128)))
    lcol[...] = jnp.broadcast_to(jnp.log(column_totals[...].astype(F32)), (8, NC))

    def prepare(first, last):
        def one(i, carry):
            slot = i % SLOTS
            strip(i, slot).wait()

            def inner(t, carry):
                t8 = pl.multiple_of(t * 8, 8)
                r0 = pl.multiple_of(i * STRIP + t * 8, 8)
                lr = lrow[pl.ds(r0, 8), :]
                for q in range(NC // 128):
                    at = slice(q * 128, (q + 1) * 128)
                    n = cbuf[slot, pl.ds(t8, 8), at].astype(F32)
                    m = jnp.maximum(n, 1.0)
                    seen = n > 0
                    B[pl.ds(r0, 8), at] = jnp.where(seen, jnp.log(m), SHIFT * LN2) - lr - lcol[:, at]
                    C[pl.ds(r0, 8), at] = jnp.where(seen, (0.25 * n) * lax.rsqrt(m) + 0.1, 0.0)
                return carry

            lax.fori_loop(0, STRIP // 8, inner, 0, unroll=8)

            @pl.when(i + SLOTS < NR // STRIP)
            def _():
                strip(i + SLOTS, slot).start()

            return carry

        lax.fori_loop(first, last, one, 0)

    prepare(0, 3)
    pl.semaphore_wait(barrier, 22)

    zp, zm, zz2 = (r, col_at(lo, z + 1, core)), (r, col_at(lo, z - 1, core)), (r, col_at(lo, z + 2, core))
    lop = (r, col_at(1 - lo, z, core))
    sib = (r, col_at(lo, z, 1 - core))
    yp, ym, yy2 = (row_at(hi, y + 1), c), (row_at(hi, y - 1), c), (row_at(hi, y + 2), c)
    hip = (row_at(1 - hi, y), c)
    rf = row_at(hi, y + 2)
    qh = row_at(1 - hi, y)

    def rcopy(l, zz, which, dev):
        return remote(rows.at[l, zz, core], rows.at[l, zz, core], which, dev)

    def ccopy(q, which, dev):
        return remote(cols.at[q], cols.at[q], which, dev)

    sent = []

    def go(copy):
        copy.start()
        sent.append(copy)
        return copy

    r_partner = go(rcopy(lo, z, R_PARTNER, lop))
    r_plus = go(rcopy(lo, z, R_PLUS, zp))
    r_minus = go(rcopy(lo, z, R_MINUS, zm))
    r_far = go(rcopy(lo, z, R_FAR, zz2))
    c_partner = go(ccopy(r, C_PARTNER, hip))
    c_plus = go(ccopy(r, C_PLUS, yp))
    c_minus = go(ccopy(r, C_MINUS, ym))
    c_far = go(ccopy(r, C_FAR, yy2))
    totals = []
    for d in range(1, 8):
        totals.append(small_copy(small.at[0], small_in.at[d], d, ((r + d) % 8, c)))
        totals[-1].start()

    prepare(3, 11)
    rg[...] = jnp.zeros_like(rg)
    lacc[...] = jnp.zeros_like(lacc)
    slopes_b[...] = jnp.zeros_like(slopes_b)
    cg[...] = jnp.zeros_like(cg)

    r_partner.wait_recv()
    r_pplus = go(rcopy(1 - lo, z, R_PPLUS, zp))
    r_pminus = go(rcopy(1 - lo, z, R_PMINUS, zm))
    r_pfar = go(rcopy(1 - lo, z, R_PFAR, zz2))
    prepare(11, 14)
    r_plus.wait_recv()
    r_minus.wait_recv()
    r_far.wait_recv()
    r_sib = go(remote(rows.at[lo, :, core], rows.at[lo, :, core], R_SIB, sib))
    prepare(14, 16)
    c_partner.wait_recv()
    c_pplus = go(ccopy(qh, C_PPLUS, yp))
    c_pminus = go(ccopy(qh, C_PMINUS, ym))

    c_pfar = ccopy(rf, C_PFAR, hip)
    r_psib = remote(rows.at[1 - lo, :, core], rows.at[1 - lo, :, core], R_PSIB, sib)

    grand = small[0]
    for d in range(1, 8):
        totals[d - 1].wait_recv()
        grand = grand + small_in[d]
    log_total = jnp.log(grand[0:1, 0:1])

    def turn_rows(l):
        for zz in range(4):
            for k in range(2):
                at = pl.ds(pl.multiple_of(l * 1024 + (zz * 2 + k) * 128, 128), 128)
                rowsT[:, at] = jnp.transpose(rows[l, zz, k].astype(F32)).astype(BF16)

    r_sib.wait_recv()
    turn_rows(lo)

    def piece(conf, score, base):
        x = score - base
        t = conf * x
        g = jnp.exp2(jnp.where(conf > 0, -1e4, x) * LOG2E)
        d = g + 2.0 ** -SHIFT
        slope = (t + g * pltpu.reciprocal(d, approx=True)).astype(BF16)
        fold = (PIECE // 8, 8, 256)
        return slope, jnp.sum((t * x).reshape(fold), axis=0), jnp.sum(jnp.log2(d).reshape(fold), axis=0)

    def kind_of(u):
        return jnp.where((u == 0) | (u == 3), CROSS, jnp.where((u == 1) | (u == 2), FAR, jnp.where(u <= 6, u - 4, 5 + (u - 7) // 2)))

    def plane_of(u):
        return jnp.where((u <= 1) | ((u >= 8) & (u % 2 == 0)), lo, 1 - lo)

    def block_of(kind):
        off = jnp.where((kind == NEXT) | (kind == CROSS_NEXT), 1, jnp.where(
            (kind == LAST) | (kind == CROSS_LAST), 3, jnp.where((kind == FAR) | (kind == CROSS_FAR), 2, 0)))
        h = jnp.where((kind <= LAST) | (kind == FAR), hi, 1 - hi)
        return h * 4 + (y + off) % 4

    def row_base(l, q):
        return pl.multiple_of(l * 1024 + q * TILE, TILE)

    def do_scores(dst, l, q, blk):
        tile = rows[l, 2 * q:2 * q + 2].reshape(TILE, K)
        dst[...] = lax.dot_general(
            tile, cols[blk], (((1,), (1,)), ((), ())), preferred_element_type=F32) - log_total

    def elementwise(src, dst, l, q, c0):
        la = jnp.zeros((8, 256), F32)
        lb = jnp.zeros((8, 256), F32)
        for v in range(TILE // PIECE):
            at = slice(v * PIECE, (v + 1) * PIECE)
            ra = pl.ds(pl.multiple_of(l * 1024 + q * TILE + v * PIECE, PIECE), PIECE)
            dst[at], a, b = piece(C[ra, pl.ds(c0, 256)], src[at], B[ra, pl.ds(c0, 256)])
            la = la + a
            lb = lb + b
        lacc[...] += la * 0.5 + (lb + float(SHIFT * TILE // 8)) * LN2

    def gradients(src, l, q, blk, kind):
        at = pl.ds(row_base(l, q), TILE)
        rg[at, :] += jnp.dot(src[...], cols[blk], preferred_element_type=F32)
        cg[kind] += jnp.dot(rowsT[:, at], src[...], preferred_element_type=F32)

    S_FAR, S_NEXT_RELAY, S_LAST_RELAY, S_CROSS_FAR, S_CROSS, S_NEXT, S_LAST = range(7)
    col_dest = [rf, row_at(hi, y + 1), row_at(hi, y - 1), row_at(1 - hi, y + 2), qh, row_at(hi, y + 1), row_at(hi, y - 1)]

    def col_copy(j):
        return remote(csend.at[j], cpart.at[j], G_COLS + j, (col_dest[j], c))

    def send_cols(j, value):
        csend[j] = value.astype(BF16)
        col_copy(j).start()

    OFFS = (2, 1, 3, 0)

    def rg_block(l, off, k):
        p = l * 4 + (z + off) % 4
        return rg[pl.ds(pl.multiple_of((p * 2 + k) * 128, 128), 128), :]

    sib_batch = remote(rsend.at[0:4], rsib.at[0:4], G_SIB, sib)

    def sib_copy(i):
        return remote(rsend.at[i], rsib.at[i], G_SIB + i, sib)

    def row_copy(i):
        dev = lop if i == 3 else (r, col_at(lo, z + OFFS[i % 4], core))
        return remote(rsum.at[i], rpart.at[i], G_ROWS + i, dev)

    def send_rows(i, value):
        rsum[i] = value.astype(BF16)
        row_copy(i).start()

    def at_step(u):
        return plane_of(u), block_of(kind_of(u)), kind_of(u)

    def tile_scores(dst, u, q):
        l, blk, _ = at_step(u)
        do_scores(dst, l, q, blk)

    def tile_slopes(src, dst, u, q):
        l, blk, _ = at_step(u)
        elementwise(src, dst, l, q, pl.multiple_of(blk * 256, 256))

    def tile_gradients(src, u, q):
        l, blk, kind = at_step(u)
        gradients(src, l, q, blk, kind)

    c_far.wait_recv()
    c_pfar.start()
    r_pplus.wait_recv()
    r_pminus.wait_recv()
    r_pfar.wait_recv()
    r_psib.start()
    tile_scores(scores_a, 0, 0)
    tile_scores(scores_b, 0, 1)
    tile_slopes(scores_a, slopes_a, 0, 0)
    tile_scores(scores_a, 1, 0)
    tile_slopes(scores_b, slopes_b, 0, 1)
    tile_gradients(slopes_a, 0, 0)
    tile_scores(scores_b, 1, 1)
    tile_slopes(scores_a, slopes_a, 1, 0)
    tile_gradients(slopes_b, 0, 1)
    tile_slopes(scores_b, slopes_b, 1, 1)
    tile_gradients(slopes_a, 1, 0)
    r_psib.wait_recv()
    c_plus.wait_recv()
    c_minus.wait_recv()
    turn_rows(1 - lo)
    tile_scores(scores_a, 2, 0)

    def run_if(test):
        return (lambda body: body()) if test else (lambda body: None)

    def steps(m, carry):
        u = m * 2

        @run_if(m == 2)
        def _():
            send_cols(S_FAR, cg[FAR])

        @run_if(m == 3)
        def _():
            c_pminus.wait_recv()

        @run_if(m == 4)
        def _():
            c_pplus.wait_recv()

        @run_if(m == 5)
        def _():
            send_cols(S_NEXT_RELAY, cg[CROSS_NEXT])
            c_pfar.wait_recv()

        tile_scores(scores_b, u, 1)
        tile_slopes(scores_a, slopes_a, u, 0)
        tile_gradients(slopes_b, u - 1, 1)
        tile_scores(scores_a, u + 1, 0)
        tile_slopes(scores_b, slopes_b, u, 1)
        tile_gradients(slopes_a, u, 0)
        tile_scores(scores_b, u + 1, 1)
        tile_slopes(scores_a, slopes_a, u + 1, 0)
        tile_gradients(slopes_b, u, 1)
        tile_scores(scores_a, u + 2, 0)
        tile_slopes(scores_b, slopes_b, u + 1, 1)
        tile_gradients(slopes_a, u + 1, 0)
        return carry

    for m in range(1, 6):
        steps(m, 0)

    send_cols(S_LAST_RELAY, cg[CROSS_LAST])
    tile_scores(scores_b, 12, 1)
    tile_slopes(scores_a, slopes_a, 12, 0)
    tile_gradients(slopes_b, 11, 1)
    for i in range(4):
        rsend[i] = rg_block(1 - lo, OFFS[i], 1 - core).astype(BF16)
    sib_batch.start()
    tile_slopes(scores_b, slopes_b, 12, 1)
    tile_gradients(slopes_a, 12, 0)

    qcols = [r, row_at(hi, y + 1), row_at(hi, y - 1)]
    for h in range(3):
        colsq[h * 256:(h + 1) * 256] = cols[qcols[h]]
        cgq[:, h * 256:(h + 1) * 256] = cg[h]

    def chip_of(t):
        off = jnp.where(t == 0, 2, jnp.where(t == 1, 1, jnp.where(t == 2, 3, 0)))
        return (z + off) % 4

    def q_rows(t, v, size):
        return pl.ds(pl.multiple_of(lo * 1024 + chip_of(t) * 256 + v, size), size)

    def q_scores(dst, t):
        tile = rows[lo, chip_of(t)].reshape(256, K)
        dst[...] = lax.dot_general(
            tile, colsq[...], (((1,), (1,)), ((), ())), preferred_element_type=F32) - log_total

    def q_elementwise(src, dst, t):
        la = jnp.zeros((8, 256), F32)
        lb = jnp.zeros((8, 256), F32)
        for h in range(3):
            c0 = pl.multiple_of(qcols[h] * 256, 256)
            for v in range(256 // PIECE):
                at = slice(v * PIECE, (v + 1) * PIECE)
                to = slice(h * 256, (h + 1) * 256)
                ra = q_rows(t, v * PIECE, PIECE)
                dst[at, to], a, b = piece(C[ra, pl.ds(c0, 256)], src[at, to], B[ra, pl.ds(c0, 256)])
                la = la + a
                lb = lb + b
        lacc[...] += la * 0.5 + (lb + float(SHIFT * WIDTH // 8)) * LN2

    def q_gradients(src, t):
        at = q_rows(t, 0, 256)
        rg[at, :] += jnp.dot(src[...], colsq[...], preferred_element_type=F32)
        cgq[...] += jnp.dot(rowsT[:, at], src[...], preferred_element_type=F32)

    def to_sibling(t):
        rsend[4 + t] = rg_block(lo, OFFS[t], 1 - core).astype(BF16)
        sib_copy(4 + t).start()

    def to_owner(t):
        sib_copy(4 + t).wait_recv()
        send_rows(4 + t, rg_block(lo, OFFS[t], core) + rsib[4 + t].astype(F32))

    tile_gradients(slopes_b, 12, 1)
    q_scores(sq_a, 0)
    send_cols(S_CROSS_FAR, cg[CROSS_FAR])
    sib_batch.wait_recv()
    for i in range(3):
        send_rows(i, rg_block(1 - lo, OFFS[i], core) + rsib[i].astype(F32))

    q_scores(sq_b, 1)
    q_elementwise(sq_a, tq_a, 0)
    q_scores(sq_a, 2)
    q_elementwise(sq_b, tq_b, 1)
    q_gradients(tq_a, 0)
    to_sibling(0)
    q_scores(sq_b, 3)
    q_elementwise(sq_a, tq_a, 2)
    q_gradients(tq_b, 1)
    to_sibling(1)
    to_owner(0)
    q_elementwise(sq_b, tq_b, 3)
    q_gradients(tq_a, 2)
    to_sibling(2)
    to_owner(1)
    small[1] = jnp.broadcast_to(
        jnp.sum(jnp.sum(lacc[...], axis=0, keepdims=True), axis=1, keepdims=True), (8, 128))
    losses = []
    for d in range(1, 8):
        losses.append(small_copy(small.at[1], small_row.at[d], 7 + d, ((r + d) % 8, c)))
        losses[-1].start()
    q_gradients(tq_b, 3)
    send_cols(S_NEXT, cgq[:, 256:512])
    send_cols(S_LAST, cgq[:, 512:768])
    to_sibling(3)
    to_owner(2)

    col_copy(S_NEXT_RELAY).wait_recv()
    col_copy(S_LAST_RELAY).wait_recv()
    send_cols(S_CROSS, cg[CROSS] + cpart[S_NEXT_RELAY].astype(F32) + cpart[S_LAST_RELAY].astype(F32))
    grad = rg_block(1 - lo, 0, core) + rsib[3].astype(F32)
    for i in range(3):
        row_copy(i).wait_recv()
        grad = grad + rpart[i].astype(F32)
    send_rows(3, grad)

    loss = small[1]
    for d in range(1, 8):
        losses[d - 1].wait_recv()
        loss = loss + small_row[d]
    small[2] = loss
    for d in range(1, 16):
        losses.append(small_copy(small.at[2], small_col.at[d], 14 + d, (r, (c + d) % 16)))
        losses[-1].start()

    sib_copy(7).wait_recv()
    grad = rg_block(lo, 0, core) + rsib[7].astype(F32)
    for i in range(4, 7):
        row_copy(i).wait_recv()
        grad = grad + rpart[i].astype(F32)
    total = cgq[:, 0:256]
    for j in (S_FAR, S_NEXT, S_LAST, S_CROSS_FAR, S_CROSS):
        col_copy(j).wait_recv()
        total = total + cpart[j].astype(F32)
    column_grad[...] = jnp.transpose(total)
    row_copy(3).wait_recv()
    row_grad[...] = grad + rpart[3].astype(F32)

    loss = small[2]
    for d in range(1, 16):
        losses[6 + d].wait_recv()
        loss = loss + small_col[d]
    mean_loss[...] = loss * (1.0 / 536870912.0)

    for copy in sent + totals + losses + [c_pfar, r_psib, sib_batch]:
        copy.wait_send()
    for j in range(7):
        col_copy(j).wait_send()
    for i in range(4, 8):
        sib_copy(i).wait_send()
    for i in range(7):
        row_copy(i).wait_send()


def update(
    row_grad, column_grad, loss, row_vectors, column_vectors, row_squares, column_squares,
    new_rows, new_columns, squares_row, squares_column, mean_loss,
):
    g = row_grad[...]
    s = row_squares[...] + g * g
    squares_row[...] = s
    new_rows[...] = row_vectors[...] - g * lax.rsqrt(s)
    g = column_grad[...]
    s = column_squares[...] + g * g
    squares_column[...] = s
    new_columns[...] = column_vectors[...] - g * lax.rsqrt(s)
    mean_loss[0, 0] = loss[0, 0]


def on_device(
    counts, row_totals, column_totals, row_vectors, column_vectors, row_squares, column_squares
):
    vmem = pl.BlockSpec(memory_space=pltpu.VMEM)
    smem = pl.BlockSpec(memory_space=pltpu.SMEM)
    row_grad, column_grad, loss = pl.pallas_call(
        kernel,
        out_shape=[
            jax.ShapeDtypeStruct((128, K), F32),
            jax.ShapeDtypeStruct((256, K), F32),
            jax.ShapeDtypeStruct((8, 128), F32),
        ],
        in_specs=[pl.BlockSpec(memory_space=pl.ANY)] + [vmem] * 4,
        out_specs=[vmem] * 3,
        scratch_shapes=[
            pltpu.VMEM((SLOTS, STRIP, NC), jnp.int32),
            pltpu.VMEM((NR, 128), F32),
            pltpu.VMEM((8, NC), F32),
            pltpu.VMEM((NR, NC), F32),
            pltpu.VMEM((NR, NC), F32),
            pltpu.VMEM((2, 4, 2, 128, K), BF16),
            pltpu.VMEM((K, NR), BF16),
            pltpu.VMEM((8, 256, K), BF16),
            pltpu.VMEM((WIDTH, K), BF16),
            pltpu.VMEM((NR, K), F32),
            pltpu.VMEM((8, K, 256), F32),
            pltpu.VMEM((K, WIDTH), F32),
            pltpu.VMEM((TILE, 256), BF16),
            pltpu.VMEM((TILE, 256), BF16),
            pltpu.VMEM((TILE, 256), F32),
            pltpu.VMEM((TILE, 256), F32),
            pltpu.VMEM((256, WIDTH), F32),
            pltpu.VMEM((256, WIDTH), F32),
            pltpu.VMEM((256, WIDTH), BF16),
            pltpu.VMEM((256, WIDTH), BF16),
            pltpu.VMEM((8, 256), F32),
            pltpu.VMEM((7, K, 256), BF16),
            pltpu.VMEM((7, K, 256), BF16),
            pltpu.VMEM((8, 128, K), BF16),
            pltpu.VMEM((8, 128, K), BF16),
            pltpu.VMEM((8, 128, K), BF16),
            pltpu.VMEM((8, 128, K), BF16),
            pltpu.VMEM((3, 8, 128), F32),
            pltpu.VMEM((8, 8, 128), F32),
            pltpu.VMEM((8, 8, 128), F32),
            pltpu.VMEM((16, 8, 128), F32),
            pltpu.SemaphoreType.DMA((SLOTS,)),
            pltpu.SemaphoreType.DMA((N_SEMS,)),
            pltpu.SemaphoreType.DMA((N_SEMS,)),
            pltpu.SemaphoreType.DMA((32,)),
            pltpu.SemaphoreType.DMA((32,)),
        ],
        compiler_params=pltpu.CompilerParams(
            collective_id=0, has_side_effects=True, vmem_limit_bytes=63 * 1024 * 1024),
        name="swivel_step",
    )(counts, row_totals.reshape(16, 128), column_totals.reshape(1, NC), row_vectors, column_vectors)
    outs = pl.pallas_call(
        update,
        out_shape=[
            jax.ShapeDtypeStruct((128, K), F32),
            jax.ShapeDtypeStruct((256, K), F32),
            jax.ShapeDtypeStruct((128, K), F32),
            jax.ShapeDtypeStruct((256, K), F32),
            jax.ShapeDtypeStruct((1, 1), F32),
        ],
        in_specs=[vmem, vmem, smem] + [vmem] * 4,
        out_specs=[vmem] * 4 + [smem],
        name="adagrad_update",
    )(row_grad, column_grad, loss, row_vectors, column_vectors, row_squares, column_squares)
    return outs[0], outs[1], outs[2], outs[3], outs[4].reshape(())


def solution(mesh):
    in_specs = (
        P("row", "col"),
        P("row"),
        P("col"),
        P(("row", "col"), None),
        P(("col", "row"), None),
        P(("row", "col"), None),
        P(("col", "row"), None),
    )
    out_specs = (
        P(("row", "col"), None),
        P(("col", "row"), None),
        P(("row", "col"), None),
        P(("col", "row"), None),
        P(),
    )
    return jax.shard_map(
        on_device, mesh=mesh, in_specs=in_specs, out_specs=out_specs, check_vma=False
    )
```

profile of v0, /device:TPU:1, one launch (start us, length us, event | category | flops | bytes accessed | tf_op | source)
XLA Modules:
  0.0 48.2 jit_solution(13943979300849734035)
XLA Ops:
  0.6 45.3 %swivel_step.1 = (f32[128,256]{1,0:T(8,128)}, f32[256,256]{1,0:T(8,128)}, f32[8,128]{1,0:T(8,128)}) custom-call(s32[2048,2048]{1,0:T(8,128)} %counts.1, s32[16,128]{1,0:T(8,128)} %bitcast.3, s32[1,2048]{1,0:T(1,128)} %bitcast.4, f32[128,256]{1,0:T(8,128)} %row_vectors.3, f32[256,256]{1,0:T(8,128)} %column_vectors.3), custom_call_target="tpu_custom_call" | custom-call | tf_op jit(solution)/shard_map/swivel_step/pallas_call | solution.py:492
  45.9 2.2 %adagrad_update.1 = (f32[128,256]{1,0:T(8,128)}, f32[256,256]{1,0:T(8,128)}, f32[128,256]{1,0:T(8,128)}, f32[256,256]{1,0:T(8,128)}, f32[1,1]{1,0:T(1,128)}) custom-call(f32[128,256]{1,0:T(8,128)} %get-tuple-element.13.row_grad, f32[256,256]{1,0:T(8,128)} %get-tuple-element.14.column_grad, f32[8,128]{1,0:T(8,128)} %get-tuple-element.15.loss, ...), custom_call_target="tpu_custom_call" | custom-call | tf_op jit(solution)/shard_map/adagrad_update/pallas_call | solution.py:543
where the time goes:
time: 48.4 us; the launch traced here: 48.2 us
  Pallas kernels  47.4 us (98%)
  between operations  0.8 us (2%)
    pallas_call x1, Pallas kernels, on_device(): pl.pallas_call(kernel, out_shape=[jax.ShapeDtypeStruct((128, K), F32), ja...  45.3 us
    pallas_call x1, Pallas kernels, on_device(): pl.pallas_call(update, out_shape=[jax.ShapeDtypeStruct((128, K), F32), ja...  2.17 us

commit v1 on v0

--- a/solution.py
+++ b/solution.py
@@ -29,12 +29,12 @@
 
 
 def kernel(
-    counts, row_totals, column_totals, row_vectors, column_vectors,
+    counts, row_totals_in, column_totals_in, row_vectors_in, column_vectors_in,
     row_grad, column_grad, mean_loss,
-    cbuf, lrow, lcol, B, C, rows, rowsT, cols, colsq, rg, cg, cgq, slopes_a, slopes_b, scores_a, scores_b,
+    row_totals, column_totals, row_vectors, column_vectors, cbuf, lrow, lcol, B, C, rows, rowsT, cols, colsq, rg, cg, cgq, slopes_a, slopes_b, scores_a, scores_b,
     sq_a, sq_b, tq_a, tq_b, lacc,
     csend, cpart, rsend, rsib, rsum, rpart, small, small_in, small_row, small_col,
-    csem, ssem, rsem, small_s, small_r,
+    csem, isem, ssem, rsem, small_s, small_r,
 ):
     r = lax.axis_index("row")
     c = lax.axis_index("col")
@@ -61,14 +61,21 @@
         return pltpu.make_async_copy(
             counts.at[pl.ds(pl.multiple_of(i * STRIP, STRIP), STRIP)], cbuf.at[slot], csem.at[slot])
 
-    for s in range(SLOTS):
-        strip(s, s).start()
-
     barrier = pltpu.get_barrier_semaphore()
     for d in range(1, 8):
         pl.semaphore_signal(barrier, inc=1, device_id=((r + d) % 8, c), device_id_type=pl.DeviceIdType.MESH)
     for d in range(1, 16):
         pl.semaphore_signal(barrier, inc=1, device_id=(r, (c + d) % 16), device_id_type=pl.DeviceIdType.MESH)
+    inputs = [
+        pltpu.make_async_copy(src, dst, isem.at[i]) for i, (src, dst) in enumerate((
+            (row_totals_in, row_totals), (column_totals_in, column_totals),
+            (row_vectors_in, row_vectors), (column_vectors_in, column_vectors)))]
+    for copy in inputs:
+        copy.start()
+    for s in range(SLOTS):
+        strip(s, s).start()
+    for copy in inputs:
+        copy.wait()
 
     rows[lo, z, core] = row_vectors[...].astype(BF16)
     cols[r] = column_vectors[...].astype(BF16)
@@ -249,7 +256,8 @@
         return remote(rsend.at[i], rsib.at[i], G_SIB + i, sib)
 
     def row_copy(i):
-        dev = lop if i == 3 else (r, col_at(lo, z + OFFS[i % 4], core))
+        l = 1 - lo if i in (0, 3) else lo
+        dev = (r, col_at(l, z + OFFS[i % 4], core))
         return remote(rsum.at[i], rpart.at[i], G_ROWS + i, dev)
 
     def send_rows(i, value):
@@ -392,7 +400,7 @@
     q_scores(sq_a, 0)
     send_cols(S_CROSS_FAR, cg[CROSS_FAR])
     sib_batch.wait_recv()
-    for i in range(3):
+    for i in (1, 2, 0):
         send_rows(i, rg_block(1 - lo, OFFS[i], core) + rsib[i].astype(F32))
 
     q_scores(sq_b, 1)
@@ -426,7 +434,7 @@
     col_copy(S_LAST_RELAY).wait_recv()
     send_cols(S_CROSS, cg[CROSS] + cpart[S_NEXT_RELAY].astype(F32) + cpart[S_LAST_RELAY].astype(F32))
     grad = rg_block(1 - lo, 0, core) + rsib[3].astype(F32)
-    for i in range(3):
+    for i in (1, 2):
         row_copy(i).wait_recv()
         grad = grad + rpart[i].astype(F32)
     send_rows(3, grad)
@@ -442,7 +450,7 @@
 
     sib_copy(7).wait_recv()
     grad = rg_block(lo, 0, core) + rsib[7].astype(F32)
-    for i in range(4, 7):
+    for i in (4, 5, 6, 0):
         row_copy(i).wait_recv()
         grad = grad + rpart[i].astype(F32)
     total = cgq[:, 0:256]
@@ -496,9 +504,13 @@
             jax.ShapeDtypeStruct((256, K), F32),
             jax.ShapeDtypeStruct((8, 128), F32),
         ],
-        in_specs=[pl.BlockSpec(memory_space=pl.ANY)] + [vmem] * 4,
+        in_specs=[pl.BlockSpec(memory_space=pl.ANY)] * 5,
         out_specs=[vmem] * 3,
         scratch_shapes=[
+            pltpu.VMEM((16, 128), jnp.int32),
+            pltpu.VMEM((1, NC), jnp.int32),
+            pltpu.VMEM((128, K), F32),
+            pltpu.VMEM((256, K), F32),
             pltpu.VMEM((SLOTS, STRIP, NC), jnp.int32),
             pltpu.VMEM((NR, 128), F32),
             pltpu.VMEM((8, NC), F32),
@@ -531,6 +543,7 @@
             pltpu.VMEM((8, 8, 128), F32),
             pltpu.VMEM((16, 8, 128), F32),
             pltpu.SemaphoreType.DMA((SLOTS,)),
+            pltpu.SemaphoreType.DMA((4,)),
             pltpu.SemaphoreType.DMA((N_SEMS,)),
             pltpu.SemaphoreType.DMA((N_SEMS,)),
             pltpu.SemaphoreType.DMA((32,)),

time: 48.4 us -> 48.8 us (level)
  Pallas kernels: 47.4 us -> 47.9 us
where the time goes in v1:
time: 48.8 us; the launch traced here: 48.7 us
  Pallas kernels  47.9 us (98%)
  between operations  0.82 us (2%)
    pallas_call x1, Pallas kernels, on_device(): pl.pallas_call(kernel, out_shape=[jax.ShapeDtypeStruct((128, K), F32), ja...  45.7 us
    pallas_call x1, Pallas kernels, on_device(): pl.pallas_call(update, out_shape=[jax.ShapeDtypeStruct((128, K), F32), ja...  2.17 us

profile of v1, /device:TPU:1, one launch (start us, length us, event | category | flops | bytes accessed | tf_op | source)
XLA Modules:
  0.0 48.7 jit_solution(2798835780253713074)
XLA Ops:
  0.6 45.7 %swivel_step.1 = (f32[128,256]{1,0:T(8,128)}, f32[256,256]{1,0:T(8,128)}, f32[8,128]{1,0:T(8,128)}) custom-call(s32[2048,2048]{1,0:T(8,128)} %counts.1, s32[16,128]{1,0:T(8,128)} %bitcast.3, s32[1,2048]{1,0:T(1,128)} %bitcast.4, f32[128,256]{1,0:T(8,128)} %row_vectors.1, f32[256,256]{1,0:T(8,128)} %column_vectors.1), custom_call_target="tpu_custom_call" | custom-call | tf_op jit(solution)/shard_map/swivel_step/pallas_call | solution.py:500
  46.4 2.2 %adagrad_update.1 = (f32[128,256]{1,0:T(8,128)}, f32[256,256]{1,0:T(8,128)}, f32[128,256]{1,0:T(8,128)}, f32[256,256]{1,0:T(8,128)}, f32[1,1]{1,0:T(1,128)}) custom-call(f32[128,256]{1,0:T(8,128)} %get-tuple-element.13.row_grad, f32[256,256]{1,0:T(8,128)} %get-tuple-element.14.column_grad, f32[8,128]{1,0:T(8,128)} %get-tuple-element.15.loss, ...), custom_call_target="tpu_custom_call" | custom-call | tf_op jit(solution)/shard_map/adagrad_update/pallas_call | solution.py:556
